TPU v7x, 32 devices: a whole 2x2x4 slice. The times are simulated.
32 devices in a mesh: parts: 2 (over y), row: 4 (over z), col: 2 (over x), sub: 2 (over core).
Axes of the slice: x: 2, y: 2, z: 4, core: 2. Of those that a mesh axis runs over, the one named last changes fastest.
Arguments:
- ancestor_cov: float32 [64, 32, 256, 256], P(('parts', 'row'), 'col'), parts along dimension 0, may hold values from -6 to 6
- owner_slot: int32 [64], P('parts'), parts along dimension 0, may hold values from 0 to 31, each once
- parent_pattern: int32 [8, 12], P(('parts', 'sub')), parts along dimension 0, may hold values from 0 to 31, as said below
- parent_factor: float32 [8, 12, 256, 256], P(('parts', 'sub'), None, 'row'), parts along dimension 0, may hold values from -0.109375 to 0.109375
- parent_inverse: float32 [8, 256, 256], P(('parts', 'sub')), parts along dimension 0, may hold values from -6 to 6
- child_parent: int32 [8], P(('parts', 'sub')), parts along dimension 0, may hold values from 0 to 1
- child_pattern: int32 [8, 8], P(('parts', 'sub')), parts along dimension 0, may hold values from 0 to 11, as said below
- child_factor: float32 [8, 9, 256, 256], P(('parts', 'sub'), None, 'row'), parts along dimension 0, may hold values from -0.125 to 0.125
- child_inverse: float32 [8, 256, 256], P(('parts', 'sub')), parts along dimension 0, may hold values from -6 to 6
Outputs:
- parent_cov: float32 [8, 32, 256, 256], P(('parts', 'sub'), 'row'), parts along dimension 0
- parent_diag: float32 [8, 256, 256], P(('parts', 'sub')), parts along dimension 0
- child_cov: float32 [8, 32, 256, 256], P(('parts', 'sub'), 'row'), parts along dimension 0
- child_upper: float32 [8, 256, 256], P(('parts', 'sub')), parts along dimension 0
- child_diag: float32 [8, 256, 256], P(('parts', 'sub')), parts along dimension 0
There are 2 independent parts, one for each index of `parts`. A program takes and returns all parts, laid end to end along the dimension named above; each array names one. Nothing has to cross between parts.
Inputs may be any that keep to these rules, and one draw needn't show every extreme that they name: `parent_pattern`: each row holds distinct ancestor ids. `child_pattern`: each row holds distinct positions.
All inputs are finite; a program needn't handle non-finite values.
Results may differ from a plain program's by a relative error of at most 0.0001.
Values sent between devices are 32-bit elements; how exact they have to be, the bound alone decides.
No kernel may reach another device: no remote copies, remote signals or barrier semaphores. Data moves between devices by JAX's collectives and lax.ppermute only.
A program may use at most 192 MiB of HBM per device.

v0:
```python
import jax
import jax.numpy as jnp
from jax import lax
from jax.sharding import PartitionSpec as P

HIGH = lax.Precision.HIGHEST


def pick_rows(slot_list, targets):
    return (slot_list[:, None, :] == targets[None, :, None]).astype(jnp.float32)


def choose(selector, blocks):
    return jnp.einsum("jcp,jpxy->jcxy", selector, blocks, precision=HIGH)


def per_device(
    ancestor_cov,
    owner_slot,
    parent_pattern,
    parent_factor,
    parent_inverse,
    child_parent,
    child_pattern,
    child_factor,
    child_inverse,
):
    ancestor_count = owner_slot.shape[0]
    row_slots = ancestor_cov.shape[0]
    col_slots = ancestor_cov.shape[1]
    group_count = parent_pattern.shape[0]
    pattern_len = parent_pattern.shape[1]
    ancestor_ids = jnp.arange(ancestor_count, dtype=jnp.int32)
    match = (parent_pattern[:, :, None] == ancestor_ids[None, None, :]).astype(jnp.int32)
    slots = jnp.sum(match * owner_slot[None, None, :], axis=-1)
    row_ids = lax.axis_index("row") * row_slots + jnp.arange(row_slots, dtype=jnp.int32)
    col_ids = lax.axis_index("col") * col_slots + jnp.arange(col_slots, dtype=jnp.int32)
    parent_onehot = child_parent[:, None] == jnp.arange(group_count, dtype=jnp.int32)[None, :]
    kid_parent_slots = jnp.sum(
        parent_onehot[:, :, None].astype(jnp.int32) * slots[None, :, :], axis=1
    )
    rel_match = (
        child_pattern[:, :, None] == jnp.arange(pattern_len, dtype=jnp.int32)[None, None, :]
    ).astype(jnp.int32)
    kid_slots = jnp.sum(rel_match * kid_parent_slots[:, None, :], axis=-1)
    col_one = pick_rows(slots, col_ids)
    row_one = pick_rows(slots, row_ids)
    col_two = pick_rows(kid_slots, col_ids)
    row_two = pick_rows(kid_slots, row_ids)
    full_one, full_two = (
        lax.all_gather(parent_factor, "row", axis=2, tiled=True),
        lax.all_gather(child_factor, "row", axis=2, tiled=True),
    )
    wcol_one = choose(col_one, full_one)
    wrow_one = choose(row_one, full_one)
    lead = full_two[:, 0]
    wcol_two = choose(col_two, full_two[:, 1:])
    wrow_two = choose(row_two, full_two[:, 1:])
    mask_one = jnp.sum(row_one, axis=-1)
    mask_two = jnp.sum(row_two, axis=-1)
    parent_weight = parent_onehot.astype(jnp.float32)
    partial_one = jnp.einsum("icxy,jcyz->jixz", ancestor_cov, wcol_one, precision=HIGH)
    prod_one = lax.psum(partial_one, "col")
    parent_cov = -mask_one[:, :, None, None] * prod_one
    term_one = jnp.einsum("jixy,jixz->jyz", wrow_one, prod_one, precision=HIGH)
    parent_diag = parent_inverse - lax.psum(term_one, "row")
    kid_pcov = jnp.einsum("kj,jixy->kixy", parent_weight, parent_cov, precision=HIGH)
    partial_two = jnp.einsum("icxy,kcyz->kixz", ancestor_cov, wcol_two, precision=HIGH)
    prod_two = lax.psum(partial_two, "col")
    prod_two = prod_two + jnp.einsum("kixy,kyz->kixz", kid_pcov, lead, precision=HIGH)
    upper_part = jnp.einsum("kixy,kixz->kyz", kid_pcov, wrow_two, precision=HIGH)
    diag_part = jnp.einsum("kixy,kixz->kyz", wrow_two, prod_two, precision=HIGH)
    upper_sum, diag_sum = lax.psum((upper_part, diag_part), "row")
    kid_pdiag = jnp.einsum("kj,jxy->kxy", parent_weight, parent_diag, precision=HIGH)
    child_cov = -mask_two[:, :, None, None] * prod_two
    upper = jnp.einsum("kxy,kyz->kxz", kid_pdiag, lead, precision=HIGH) + upper_sum
    child_upper = -upper
    child_diag = child_inverse - jnp.einsum("kxy,kxz->kyz", lead, upper, precision=HIGH) - diag_sum
    return (parent_cov, parent_diag, child_cov, child_upper, child_diag)


def solution(mesh):
    in_specs = (
        P(("parts", "row"), "col", None, None),
        P("parts"),
        P(("parts", "sub"), None),
        P(("parts", "sub"), None, "row", None),
        P(("parts", "sub"), None, None),
        P(("parts", "sub")),
        P(("parts", "sub"), None),
        P(("parts", "sub"), None, "row", None),
        P(("parts", "sub"), None, None),
    )
    out_specs = (
        P(("parts", "sub"), "row", None, None),
        P(("parts", "sub"), None, None),
        P(("parts", "sub"), "row", None, None),
        P(("parts", "sub"), None, None),
        P(("parts", "sub"), None, None),
    )
    return jax.shard_map(
        per_device, mesh=mesh, in_specs=in_specs, out_specs=out_specs, check_vma=False
    )
```

profile of v0, /device:TPU:0, one launch (start us, length us, event | category | flops | bytes accessed | tf_op | source)
XLA Modules:
  0.0 643.6 jit_solution(5882674542085067443)
XLA Ops:
  7.2 2.4 copy.35
  9.7 0.7 all-gather.3.cloned.1.call-update
  11.1 35.0 %copy.54 = f32[8,16,256,256,1]{2,1,3,0,4:T(8,128)} copy(f32[8,16,256,256,1]{3,2,1,0,4:T(8,128)} %bitcast.92) | data formatting | bytes 67108864 | tf_op args[0]
  46.4 56.0 %all-gather.5.cloned.1.call-done = f32[2,9,256,256]{3,2,0,1:T(8,128)} async-done(((f32[2,9,64,256]{3,2,0,1:T(8,128)}), f32[2,9,256,256]{3,2,0,1:T(8,128)}) %all-gather.5.cloned.1.call-update) | async-done | bytes 4718608 | tf_op jit(solution)/shard_map/all_gather | solution.py:52
  102.3 2.6 slice.9
  105.0 2.1 copy-done
  107.1 5.8 fusion.12
  112.9 62.4 %fusion.22 = f32[2,8,256,256]{2,3,1,0:T(8,128)} fusion(f32[8,16,256,256,1]{2,1,3,0,4:T(8,128)} %copy.54, f32[2,16,256,256]{3,1,2,0:T(8,128)S(1)} %fusion.12), kind=kOutput, calls=%fused_computation.18 | convolution fusion | flops 51539607552 | bytes 46137344 | tf_op jit(solution)/shard_map/icxy,kcyz->kixz/dot_general | solution.py:68
  175.3 42.4 %all-gather.3.cloned.1.call-done = f32[2,12,256,256]{3,2,1,0:T(8,128)} async-done(((f32[2,12,64,256]{3,2,1,0:T(8,128)}), f32[2,12,256,256]{3,2,1,0:T(8,128)}) %all-gather.3.cloned.1.call-update) | async-done | bytes 6291472 | tf_op jit(solution)/shard_map/all_gather | solution.py:51
  217.7 10.7 %fusion.2 = f32[2,16,256,256]{3,1,2,0:T(8,128)S(1)} fusion(f32[2,12,256,256]{3,2,1,0:T(8,128)} %all-gather.3.cloned.1.call-done, s32[2,12]{1,0:T(2,128)S(1)} %copy.31, s32[16]{0:T(128)S(1)} %iota_add_fusion), kind=kOutput, calls=%fused_computation.2 | convolution fusion | flops 301990272 | bytes 14680224 | tf_op jit(solution)/shard_map/jcp,jpxy->jcxy/dot_general | solution.py:14
  228.4 62.5 %fusion.19 = f32[2,8,256,256]{2,3,1,0:T(8,128)} fusion(f32[8,16,256,256,1]{2,1,3,0,4:T(8,128)} %copy.54, f32[2,16,256,256]{3,1,2,0:T(8,128)S(1)} %fusion.2), kind=kOutput, calls=%fused_computation.17 | convolution fusion | flops 51539607552 | bytes 46137344 | tf_op jit(solution)/shard_map/icxy,jcyz->jixz/dot_general | solution.py:62
  291.2 0.4 copy-done.12
  291.8 8.7 %fusion.14 = f32[2,8,256,256]{3,1,2,0:T(8,128)} fusion(f32[2,8,256,256]{3,2,0,1:T(8,128)} %copy-done, s32[2,8]{1,0:T(2,128)S(1)} %copy-done.12, s32[8]{0:T(128)S(1)} %iota_add_fusion.1), kind=kOutput, calls=%fused_computation.14 | convolution fusion | flops 100663424 | bytes 8388704 | tf_op jit(solution)/shard_map/jcp,jpxy->jcxy/dot_general | solution.py:14
  300.5 7.4 %fusion = f32[2,8,256,256]{3,1,2,0:T(8,128)} fusion(f32[2,12,256,256]{3,2,1,0:T(8,128)S(1)} %bitcast.91, s32[2,12]{1,0:T(2,128)S(1)} %copy.31, s32[8]{0:T(128)S(1)} %iota_add_fusion.1), kind=kOutput, calls=%fused_computation | convolution fusion | flops 150995136 | bytes 10485888 | tf_op jit(solution)/shard_map/jcp,jpxy->jcxy/dot_general | solution.py:14
  307.8 180.0 %all-reduce.7.cloned.1.call-done = (f32[2,8,256,256]{2,3,1,0:T(8,128)}, f32[2,8,256,256]{2,3,1,0:T(8,128)}) async-done(((f32[2,8,256,256]{2,3,1,0:T(8,128)}, f32[2,8,256,256]{2,3,1,0:T(8,128)}), (f32[2,8,256,256]{2,3,1,0:T(8,128)}, f32[2,8,256,256]{2,3,1,0:T(8,128)})) %all-reduce.7.cloned.1.call-update) | async-done | bytes 8388624 | tf_op jit(solution)/shard_map/psum | solution.py:63
  487.9 5.4 copy.59
  493.3 4.7 broadcast_multiply_fusion.1
  498.0 7.3 %copy.36 = f32[2,8,256,256]{3,0,2,1:T(2,128)} copy(f32[2,8,256,256]{2,3,1,0:T(8,128)} %broadcast_multiply_fusion.1) | data formatting | bytes 8388608 | tf_op jit(solution)/shard_map/mul | solution.py:64
  505.3 10.2 %fusion.54 = f32[2,8,256,256]{3,0,2,1:T(2,128)S(1)} fusion(f32[2,8,256,256]{3,0,2,1:T(2,128)} %copy.36, s32[2]{0:T(128)S(1)} %copy-done.14), kind=kOutput, calls=%fused_computation.60 | convolution fusion | flops 25165828 | bytes 8388616 | tf_op jit(solution)/shard_map/kj,jixy->kixy/dot_general | solution.py:67
  515.5 7.9 %broadcast_multiply_fusion = (f32[2,8,256,256]{2,3,1,0:T(8,128)}, f32[2,8,256,256]{2,3,1,0:T(8,128)}) fusion(f32[2,8]{1,0:T(2,128)S(1)} %neg.20, f32[2,8,256,256]{2,3,1,0:T(8,128)S(1)} %copy-done.4, f32[2,9,256,256]{3,2,0,1:T(8,128)} %all-gather.5.cloned.1.call-done, f32[2,8,256,256]{3,0,2,1:T(2,128)S(1)} %fusion.54), kind=kOutput, calls=%fused_computation.19 | convolution fusion | flops 3223322624 | bytes 17301568 | tf_op jit(solution)/shard_map/kixy,kyz->kixz/dot_general | solution.py:70
  523.4 5.8 copy.76
  529.3 12.9 %fusion.27 = f32[2,256,256]{2,1,0:T(8,128)} fusion(f32[2,8,256,256]{3,1,2,0:T(8,128)} %fusion.14, f32[2,8,256,256]{3,0,2,1:T(2,128)} %copy-done.1), kind=kOutput, calls=%fused_computation.26 | convolution fusion | flops 3221225472 | bytes 8912896 | tf_op jit(solution)/shard_map/kixy,kixz->kyz/dot_general | solution.py:71
  542.2 8.0 %convolution_bitcast_fusion = f32[2,256,256]{1,2,0:T(8,128)} fusion(f32[2,8,256,256]{3,1,2,0:T(8,128)S(1)} %copy-done.2, f32[2,8,256,256]{3,1,2,0:T(8,128)S(1)} %copy-done.3), kind=kOutput, calls=%fused_computation.21 | convolution fusion | flops 3221225472 | bytes 8912896 | tf_op jit(solution)/shard_map/kixy,kixz->kyz/dot_general | solution.py:72
  550.3 7.9 %convolution_bitcast_fusion.2 = f32[2,256,256]{2,1,0:T(8,128)} fusion(f32[2,8,256,256]{3,1,2,0:T(8,128)S(1)} %copy-done.5, f32[2,8,256,256]{3,1,2,0:T(8,128)S(1)} %copy-done.6), kind=kOutput, calls=%fused_computation.27 | convolution fusion | flops 3221225472 | bytes 8912896 | tf_op jit(solution)/shard_map/jixy,jixz->jyz/dot_general | solution.py:65
  558.4 5.4 copy.47
  563.8 5.6 copy.48
  569.4 59.2 %all-reduce.5.cloned.1.call-done = (f32[2,256,256]{2,1,0:T(8,128)}, f32[2,256,256]{2,1,0:T(8,128)}, f32[2,256,256]{1,2,0:T(8,128)}) async-done(((f32[2,256,256]{2,1,0:T(8,128)}, f32[2,256,256]{2,1,0:T(8,128)}, f32[2,256,256]{1,2,0:T(8,128)}), (f32[2,256,256]{2,1,0:T(8,128)}, f32[2,256,256]{2,1,0:T(8,128)}, f32[2,256,256]{1,2,0:T(8,128)})) %all-reduce.5.cloned.1.call-update) | async-done | bytes 1572880 | tf_op jit(solution)/shard_map/psum | solution.py:66
  628.6 1.2 sub.9
  629.8 1.3 fusion.34
  631.1 2.7 fusion.60
  633.7 2.1 fusion.26
  635.8 1.0 copy.49
  (59 shorter events, 1.7 us)
Async XLA Ops:
  7.2 3.3 copy-start.15
  7.2 3.4 copy-start.17
  7.2 3.8 copy-start.13
  7.2 95.1 %all-gather.5.cloned.1.call-start = ((), (), s32[]{:S(2)}) async-start(), calls=%async_computation.1 | async-start | bytes 5898240 | tf_op jit(solution)/shard_map/all_gather | solution.py:52
  9.7 208.0 %all-gather.3.cloned.1.call-start = ((), (), s32[]{:S(2)}) async-start(), calls=%async_computation | async-start | bytes 7864320 | tf_op jit(solution)/shard_map/all_gather | solution.py:51
  10.4 477.4 %all-reduce.7.cloned.1.call-start = ((), (), s32[]{:S(2)}) async-start(), calls=%async_computation.3 | async-start | bytes 16777216 | tf_op jit(solution)/shard_map/psum | solution.py:63
  11.1 35.0 %copy-start.16 = (s32[2,8]{1,0:T(2,128)S(1)}, s32[2,8]{1,0:T(2,128)}, u32[]{:S(2)}) copy-start(s32[2,8]{1,0:T(2,128)} %param.15) | copy-start | bytes 196
  46.3 58.6 %copy-start.11 = (s32[2,8]{1,0:T(2,128)}, s32[2,8]{1,0:T(2,128)S(1)}, u32[]{:S(2)}) copy-start(s32[2,8]{1,0:T(2,128)S(1)} %select_reduce_fusion) | copy-start | bytes 196
  105.0 2.1 copy-start
  290.9 0.7 copy-start.12
  290.9 9.6 %slice-start = ((s8[6291456]{0:T(1024)(128)(4,1)}), s8[2097152]{0:T(1024)(128)(4,1)S(1)}, s32[]{:S(2)}) async-start(s8[6291456]{0:T(1024)(128)(4,1)} %bitcast.90), calls=%async_computation.4 | async-start | bytes 4194304
  291.0 337.6 %all-reduce.5.cloned.1.call-start = ((), (), s32[]{:S(2)}) async-start(), calls=%async_computation.2 | async-start | bytes 3145728 | tf_op jit(solution)/shard_map/psum | solution.py:66
  291.0 9.5 %slice-start.1 = ((s8[6291456]{0:T(1024)(128)(4,1)}), s8[4194304]{0:T(1024)(128)(4,1)S(1)}, s32[]{:S(2)}) async-start(s8[6291456]{0:T(1024)(128)(4,1)} %bitcast.90), calls=%async_computation.5 | async-start | bytes 8388608
  498.0 7.3 %copy-start.14 = (s32[2]{0:T(128)S(1)}, s32[2]{0:T(128)}, u32[]{:S(2)}) copy-start(s32[2]{0:T(128)} %param.14) | copy-start | bytes 28
  505.3 10.3 %copy-start.4 = (f32[2,8,256,256]{2,3,1,0:T(8,128)S(1)}, f32[2,8,256,256]{2,3,1,0:T(8,128)}, u32[]{:S(2)}) copy-start(f32[2,8,256,256]{2,3,1,0:T(8,128)} %get-tuple-element.19) | copy-start | bytes 12582916
  515.5 7.9 %copy-start.1 = (f32[2,8,256,256]{3,0,2,1:T(2,128)}, f32[2,8,256,256]{3,0,2,1:T(2,128)S(1)}, u32[]{:S(2)}) copy-start(f32[2,8,256,256]{3,0,2,1:T(2,128)S(1)} %fusion.54) | copy-start | bytes 12582916
  529.3 13.0 %copy-start.2 = (f32[2,8,256,256]{3,1,2,0:T(8,128)S(1)}, f32[2,8,256,256]{3,1,2,0:T(8,128)}, u32[]{:S(2)}) copy-start(f32[2,8,256,256]{3,1,2,0:T(8,128)} %fusion.14) | copy-start | bytes 12582916
  529.3 12.9 %copy-start.3 = (f32[2,8,256,256]{3,1,2,0:T(8,128)S(1)}, f32[2,8,256,256]{3,1,2,0:T(8,128)}, u32[]{:S(2)}) copy-start(f32[2,8,256,256]{3,1,2,0:T(8,128)} %copy.76) | copy-start | bytes 12582916
  542.2 8.0 %copy-start.5 = (f32[2,8,256,256]{3,1,2,0:T(8,128)S(1)}, f32[2,8,256,256]{3,1,2,0:T(8,128)}, u32[]{:S(2)}) copy-start(f32[2,8,256,256]{3,1,2,0:T(8,128)} %fusion) | copy-start | bytes 12582916
  542.2 8.0 %copy-start.6 = (f32[2,8,256,256]{3,1,2,0:T(8,128)S(1)}, f32[2,8,256,256]{3,1,2,0:T(8,128)}, u32[]{:S(2)}) copy-start(f32[2,8,256,256]{3,1,2,0:T(8,128)} %copy.59) | copy-start | bytes 12582916
  550.3 7.9 %copy-start.10 = (f32[2,256,256]{2,1,0:T(8,128)S(1)}, f32[2,256,256]{2,1,0:T(8,128)}, u32[]{:S(2)}) copy-start(f32[2,256,256]{2,1,0:T(8,128)} %param.17) | copy-start | bytes 1572868
  563.8 64.8 %copy-start.8 = (f32[2,256,256]{2,1,0:T(8,128)S(1)}, f32[2,256,256]{2,1,0:T(8,128)}, u32[]{:S(2)}) copy-start(f32[2,256,256]{2,1,0:T(8,128)} %param.13) | copy-start | bytes 1572868
  628.6 5.2 copy-start.9
  629.8 7.1 %copy-start.7 = (f32[2,256,256]{2,1,0:T(8,128)}, f32[2,256,256]{2,1,0:T(8,128)S(1)}, u32[]{:S(2)}) copy-start(f32[2,256,256]{2,1,0:T(8,128)S(1)} %sub.9) | copy-start | bytes 1572868
Sparse Core Ops, SparseCore 0:
  10.2 92.0 all-gather.4
  103.9 113.7 all-gather.2
  291.1 196.7 all-reduce.6
  558.3 70.2 all-reduce.4
where the time goes:
time: 650 us; the launch traced here: 644 us
  waiting for transfers between devices  338 us (52%)
  matrix products  210 us (32%)
  local copies, waits for them, and re-layouts  73.5 us (11%)
  between operations  14.3 us (2%)
  other arithmetic  6.93 us (1%)
    psum x1, waiting for transfers between devices, per_device(): prod_one = lax.psum(partial_one, 'col')  180 us
    dot_general x1, matrix products, per_device(): jnp.einsum('icxy,jcyz->jixz', ancestor_cov, wcol_one, precision=HIGH)  62.5 us
    dot_general x1, matrix products, per_device(): jnp.einsum('icxy,kcyz->kixz', ancestor_cov, wcol_two, precision=HIGH)  62.4 us
    psum x1, waiting for transfers between devices, per_device(): parent_diag = parent_inverse - lax.psum(term_one, 'row')  59.2 us
    all_gather x1, waiting for transfers between devices, per_device(): lax.all_gather(child_factor, 'row', axis=2, tiled=True)  56 us
    unnamed x47, local copies, waits for them, and re-layouts  52.2 us
    all_gather x1, waiting for transfers between devices, per_device(): lax.all_gather(parent_factor, 'row', axis=2, tiled=True)  42.4 us
    dot_general x4, matrix products, choose(): return jnp.einsum('jcp,jpxy->jcxy', selector, blocks, precision=HIGH)  32.5 us
  transfers between devices with their start and end apart: 4, of which 4 were waited for; matrix products, arithmetic and copies ran while one was open for 21% of the time, Pallas kernels for 0%

commit v1 on v0

--- a/solution.py
+++ b/solution.py
@@ -63,7 +63,10 @@
     prod_one = lax.psum(partial_one, "col")
     parent_cov = -mask_one[:, :, None, None] * prod_one
     term_one = jnp.einsum("jixy,jixz->jyz", wrow_one, prod_one, precision=HIGH)
-    parent_diag = parent_inverse - lax.psum(term_one, "row")
+    load_rails = lambda payload, dev_axis: jnp.sum(
+        lax.all_gather(payload, axis_name=dev_axis), axis=0
+    )
+    parent_diag = parent_inverse - load_rails(term_one, "row")
     kid_pcov = jnp.einsum("kj,jixy->kixy", parent_weight, parent_cov, precision=HIGH)
     partial_two = jnp.einsum("icxy,kcyz->kixz", ancestor_cov, wcol_two, precision=HIGH)
     prod_two = lax.psum(partial_two, "col")

time: 650 us -> 730 us (1.12)
  waiting for transfers between devices: 338 us -> 410 us
    all_gather x1, waiting for transfers between devices: 56 us -> 114 us  [per_device(): lax.all_gather(child_factor, 'row', axis=2, tiled=True)]
    all_gather x1, waiting for transfers between devices: 42.4 us -> 80.3 us  [per_device(): lax.all_gather(parent_factor, 'row', axis=2, tiled=True)]
    psum x1, waiting for transfers between devices: 59.2 us -> 38.5 us  [per_device(): upper_sum, diag_sum = lax.psum((upper_part, diag_part), 'row')]
    dot_general x1, matrix products: 62.5 us -> 72.5 us  [per_device(): jnp.einsum('icxy,jcyz->jixz', ancestor_cov, wcol_one, precision=HIGH)]
    unnamed x47 -> x42, local copies, waits for them, and re-layouts: 52.2 us -> 54.5 us
  transfers between devices with their start and end apart: 4 -> 5, of which waited for: 4 -> 4; matrix products, arithmetic and copies ran while one was open for 21% -> 26% of each run, Pallas kernels for 0% -> 0%
where the time goes in v1:
time: 730 us; the launch traced here: 725 us
  waiting for transfers between devices  410 us (56%)
  matrix products  217 us (30%)
  local copies, waits for them, and re-layouts  75.3 us (10%)
  between operations  14.2 us (2%)
  other arithmetic  7.89 us (1%)
    psum x1, waiting for transfers between devices, per_device(): prod_one = lax.psum(partial_one, 'col')  177 us
    all_gather x1, waiting for transfers between devices, per_device(): lax.all_gather(child_factor, 'row', axis=2, tiled=True)  114 us
    all_gather x1, waiting for transfers between devices, per_device(): lax.all_gather(parent_factor, 'row', axis=2, tiled=True)  80.3 us
    dot_general x1, matrix products, per_device(): jnp.einsum('icxy,jcyz->jixz', ancestor_cov, wcol_one, precision=HIGH)  72.5 us
    dot_general x1, matrix products, per_device(): jnp.einsum('icxy,kcyz->kixz', ancestor_cov, wcol_two, precision=HIGH)  63.4 us
    unnamed x42, local copies, waits for them, and re-layouts  54.5 us
    psum x1, waiting for transfers between devices, per_device(): upper_sum, diag_sum = lax.psum((upper_part, diag_part), 'row')  38.5 us
    dot_general x4, matrix products, choose(): return jnp.einsum('jcp,jpxy->jcxy', selector, blocks, precision=HIGH)  29.5 us
  transfers between devices with their start and end apart: 5, of which 4 were waited for; matrix products, arithmetic and copies ran while one was open for 26% of the time, Pallas kernels for 0%

profile of v1, /device:TPU:0, one launch (start us, length us, event | category | flops | bytes accessed | tf_op | source)
XLA Modules:
  0.0 724.7 jit_solution(1218453191620871023)
XLA Ops:
  7.2 3.4 copy.54
  10.8 2.2 copy.49
  13.7 34.9 %copy.71 = f32[8,16,256,256,1]{2,1,3,0,4:T(8,128)} copy(f32[8,16,256,256,1]{3,2,1,0,4:T(8,128)} %bitcast.93) | data formatting | bytes 67108864 | tf_op args[0]
  48.9 114.3 %all-gather.7.cloned.1.call-done = f32[2,9,256,256]{3,1,2,0:T(8,128)} async-done(((f32[2,9,64,256]{3,1,2,0:T(8,128)}), f32[2,9,256,256]{3,1,2,0:T(8,128)}) %all-gather.7.cloned.1.call-update) | async-done | bytes 4718608 | tf_op jit(solution)/shard_map/all_gather | solution.py:52
  163.2 6.2 fusion.10
  169.4 63.4 %fusion.18 = f32[2,8,256,256]{2,3,1,0:T(8,128)} fusion(f32[8,16,256,256,1]{2,1,3,0,4:T(8,128)} %copy.71, f32[2,16,256,256]{3,1,2,0:T(8,128)S(1)} %fusion.10), kind=kOutput, calls=%fused_computation.14 | convolution fusion | flops 51539607552 | bytes 46137344 | tf_op jit(solution)/shard_map/icxy,kcyz->kixz/dot_general | solution.py:71
  232.8 80.3 %all-gather.5.cloned.1.call-done = f32[2,12,256,256]{3,1,2,0:T(8,128)} async-done(((f32[2,12,64,256]{3,1,2,0:T(8,128)}), f32[2,12,256,256]{3,1,2,0:T(8,128)}) %all-gather.5.cloned.1.call-update) | async-done | bytes 6291472 | tf_op jit(solution)/shard_map/all_gather | solution.py:51
  313.2 6.8 fusion.35
  320.0 72.5 %fusion.15 = f32[2,8,256,256]{2,3,1,0:T(8,128)} fusion(f32[8,16,256,256,1]{2,1,3,0,4:T(8,128)} %copy.71, f32[2,16,256,256]{3,1,2,0:T(8,128)S(1)} %fusion.35), kind=kOutput, calls=%fused_computation.13 | convolution fusion | flops 51539607552 | bytes 46137344 | tf_op jit(solution)/shard_map/icxy,jcyz->jixz/dot_general | solution.py:62
  392.7 0.6 copy-done.11
  393.6 2.5 slice.10
  396.0 8.1 %fusion.8 = f32[2,8,256,256]{3,1,2,0:T(8,128)} fusion(f32[2,9,256,256]{3,1,2,0:T(8,128)} %all-gather.7.cloned.1.call-done, s32[2,8]{1,0:T(2,128)S(1)} %copy-done.11, s32[8]{0:T(128)S(1)} %iota_add_fusion.1), kind=kOutput, calls=%fused_computation.8 | convolution fusion | flops 100663424 | bytes 8388704 | tf_op jit(solution)/shard_map/jcp,jpxy->jcxy/dot_general | solution.py:14
  404.1 8.4 %fusion.43 = f32[2,8,256,256]{3,1,2,0:T(8,128)} fusion(f32[2,12,256,256]{3,1,2,0:T(8,128)} %all-gather.5.cloned.1.call-done, s32[2,12]{1,0:T(2,128)S(1)} %copy.47, s32[8]{0:T(128)S(1)} %iota_add_fusion.1), kind=kOutput, calls=%fused_computation.48 | convolution fusion | flops 150995136 | bytes 10485888 | tf_op jit(solution)/shard_map/jcp,jpxy->jcxy/dot_general | solution.py:14
  412.5 177.0 %all-reduce.7.cloned.1.call-done = (f32[2,8,256,256]{2,3,1,0:T(8,128)}, f32[2,8,256,256]{2,3,1,0:T(8,128)}) async-done(((f32[2,8,256,256]{2,3,1,0:T(8,128)}, f32[2,8,256,256]{2,3,1,0:T(8,128)}), (f32[2,8,256,256]{2,3,1,0:T(8,128)}, f32[2,8,256,256]{2,3,1,0:T(8,128)})) %all-reduce.7.cloned.1.call-update) | async-done | bytes 8388624 | tf_op jit(solution)/shard_map/psum | solution.py:63
  589.5 5.4 copy.75
  594.9 5.0 broadcast_multiply_fusion.1
  599.9 1.2 copy-done.5
  601.2 7.9 %convolution_bitcast_fusion.2 = f32[2,256,256]{2,1,0:T(8,128)} fusion(f32[2,8,256,256]{3,1,2,0:T(8,128)S(1)} %copy-done.4, f32[2,8,256,256]{3,1,2,0:T(8,128)S(1)} %copy-done.5), kind=kOutput, calls=%fused_computation.23 | convolution fusion | flops 3221225472 | bytes 8912896 | tf_op jit(solution)/shard_map/jixy,jixz->jyz/dot_general | solution.py:65
  609.1 7.2 copy.56
  616.4 10.3 %fusion.52 = f32[2,8,256,256]{3,0,2,1:T(2,128)S(1)} fusion(f32[2,8,256,256]{3,0,2,1:T(2,128)} %copy.56, s32[2]{0:T(128)S(1)} %copy-done.13), kind=kOutput, calls=%fused_computation.58 | convolution fusion | flops 25165828 | bytes 8388616 | tf_op jit(solution)/shard_map/kj,jixy->kixy/dot_general | solution.py:70
  626.7 6.5 broadcast_multiply_fusion
  633.2 5.6 copy.64
  638.8 11.2 %convolution_bitcast_fusion = f32[2,256,256]{1,2,0:T(8,128)} fusion(f32[2,8,256,256]{3,1,2,0:T(8,128)} %fusion.8, f32[2,8,256,256]{3,1,2,0:T(8,128)} %copy.64), kind=kOutput, calls=%fused_computation.17 | convolution fusion | flops 3221225472 | bytes 8912896 | tf_op jit(solution)/shard_map/kixy,kixz->kyz/dot_general | solution.py:75
  650.1 9.6 %fusion.23 = f32[2,256,256]{2,1,0:T(8,128)} fusion(f32[2,8,256,256]{3,1,2,0:T(8,128)S(1)} %copy-done.2, f32[2,8,256,256]{3,0,2,1:T(2,128)S(1)} %copy-done.1), kind=kOutput, calls=%fused_computation.22 | convolution fusion | flops 3221225472 | bytes 8912896 | tf_op jit(solution)/shard_map/kixy,kixz->kyz/dot_general | solution.py:74
  659.9 5.4 copy.66
  665.2 5.4 copy.67
  670.7 1.8 reduce_sum.56
  672.5 1.3 fusion.30
  673.9 38.5 %all-reduce.5.cloned.1.call-done = (f32[2,256,256]{2,1,0:T(8,128)}, f32[2,256,256]{1,2,0:T(8,128)}) async-done(((f32[2,256,256]{2,1,0:T(8,128)}, f32[2,256,256]{1,2,0:T(8,128)}), (f32[2,256,256]{2,1,0:T(8,128)}, f32[2,256,256]{1,2,0:T(8,128)})) %all-reduce.5.cloned.1.call-update) | async-done | bytes 1048592 | tf_op jit(solution)/shard_map/psum | solution.py:76
  712.4 2.5 fusion.58
  714.9 2.1 fusion.22
  717.0 1.0 copy.68
  (57 shorter events, 1.8 us)
Async XLA Ops:
  7.2 3.6 copy-start.7
  7.2 156.0 %all-gather.7.cloned.1.call-start = ((), (), s32[]{:S(2)}) async-start(), calls=%async_computation.1 | async-start | bytes 10485760 | tf_op jit(solution)/shard_map/all_gather | solution.py:52
  10.7 2.4 copy-start.12
  10.7 2.5 copy-start.14
  10.7 2.6 copy-start.16
  10.7 302.5 %all-gather.5.cloned.1.call-start = ((), (), s32[]{:S(2)}) async-start(), calls=%async_computation | async-start | bytes 10485760 | tf_op jit(solution)/shard_map/all_gather | solution.py:51
  13.0 576.5 %all-reduce.7.cloned.1.call-start = ((), (), s32[]{:S(2)}) async-start(), calls=%async_computation.4 | async-start | bytes 16777216 | tf_op jit(solution)/shard_map/psum | solution.py:63
  13.7 34.9 %copy-start.15 = (s32[2,8]{1,0:T(2,128)S(1)}, s32[2,8]{1,0:T(2,128)}, u32[]{:S(2)}) copy-start(s32[2,8]{1,0:T(2,128)} %param.15) | copy-start | bytes 196
  48.9 120.5 %copy-start.10 = (s32[2,8]{1,0:T(2,128)}, s32[2,8]{1,0:T(2,128)S(1)}, u32[]{:S(2)}) copy-start(s32[2,8]{1,0:T(2,128)S(1)} %select_reduce_fusion) | copy-start | bytes 196
  392.6 0.7 copy-start.11
  392.6 278.1 %all-gather.9.cloned.1.call-start = ((), (), s32[]{:S(2)}) async-start(), calls=%async_computation.2 | async-start | bytes 2621440 | tf_op jit(solution)/shard_map/all_gather | solution.py:67
  594.9 5.0 copy-start.4
  594.9 6.2 copy-start.5
  609.1 7.3 %copy-start.13 = (s32[2]{0:T(128)S(1)}, s32[2]{0:T(128)}, u32[]{:S(2)}) copy-start(s32[2]{0:T(128)} %param.14) | copy-start | bytes 28
  609.1 103.3 %all-reduce.5.cloned.1.call-start = ((), (), s32[]{:S(2)}) async-start(), calls=%async_computation.3 | async-start | bytes 2097152 | tf_op jit(solution)/shard_map/psum | solution.py:76
  616.4 10.3 %copy-start.3 = (f32[2,8,256,256]{2,3,1,0:T(8,128)S(1)}, f32[2,8,256,256]{2,3,1,0:T(8,128)}, u32[]{:S(2)}) copy-start(f32[2,8,256,256]{2,3,1,0:T(8,128)} %get-tuple-element.23) | copy-start | bytes 12582916
  626.7 6.5 copy-start
  638.8 11.2 %copy-start.1 = (f32[2,8,256,256]{3,0,2,1:T(2,128)S(1)}, f32[2,8,256,256]{3,0,2,1:T(2,128)}, u32[]{:S(2)}) copy-start(f32[2,8,256,256]{3,0,2,1:T(2,128)} %copy-done) | copy-start | bytes 12582916
  638.8 11.2 %copy-start.2 = (f32[2,8,256,256]{3,1,2,0:T(8,128)S(1)}, f32[2,8,256,256]{3,1,2,0:T(8,128)}, u32[]{:S(2)}) copy-start(f32[2,8,256,256]{3,1,2,0:T(8,128)} %fusion.8) | copy-start | bytes 12582916
  650.0 9.6 %copy-start.9 = (f32[2,256,256]{2,1,0:T(8,128)S(1)}, f32[2,256,256]{2,1,0:T(8,128)}, u32[]{:S(2)}) copy-start(f32[2,256,256]{2,1,0:T(8,128)} %param.17) | copy-start | bytes 1572868
  665.2 7.2 copy-start.8
  672.5 45.4 %copy-start.6 = (f32[2,256,256]{2,1,0:T(8,128)}, f32[2,256,256]{2,1,0:T(8,128)S(1)}, u32[]{:S(2)}) copy-start(f32[2,256,256]{2,1,0:T(8,128)S(1)} %sub.9) | copy-start | bytes 1572868
Sparse Core Ops, SparseCore 0:
  10.8 152.3 all-gather.6
  165.3 147.8 all-gather.4
  392.7 196.7 all-reduce.6
  609.2 46.2 all-gather.8
  659.8 52.5 all-reduce.4
